TPU v7x, 32 devices: a whole 2x2x4 slice. The times are simulated.
32 devices in a mesh: img: 8 (over z, y), shot: 4 (over x, core).
Axes of the slice: x: 2, y: 2, z: 4, core: 2. Of those that a mesh axis runs over, the one named last changes fastest.
Arguments:
- shot_green: bfloat16 [2, 3584, 1024], P(None, 'img', 'shot'), may hold values from -6 to 6
- rec_green: bfloat16 [2, 3584, 3584], P(None, 'img'), may hold values from -0.0625 to 0.0625
- model: float32 [3584], P('img'), may hold values from 0.2 to 2
- hadamard_order: int32 [256], replicated, may hold values from 0 to 255, each once
- shot_signs: int32 [1024], P('shot'), may hold values from 0 to 1
Outputs:
- born_data: bfloat16 [2, 3584, 1024], P(None, 'img', 'shot')
Inputs may be any that keep to these rules, and one draw needn't show every extreme that they name: `hadamard_order`: each of 0 to 255 once.
All inputs are finite; a program needn't handle non-finite values.
Results may differ from a plain program's by a relative error of at most 0.0049.
Values may be sent and summed in bfloat16 or wider, within the bound.
A program may use at most 128 MiB of HBM per device.

v0:
```python
import jax
import jax.numpy as jnp
from jax import lax
from jax.sharding import PartitionSpec as P


def parity(values, bit_count):
    result = jnp.zeros_like(values)
    for shift_by in range(bit_count):
        result = jnp.bitwise_xor(result, jnp.bitwise_and(jnp.right_shift(values, shift_by), 1))
    return result


def on_device(shot_green, rec_green, model, hadamard_order, shot_signs):
    shot_local = shot_green.shape[2]
    x_local = shot_green.shape[1]
    blocks = lax.axis_size("shot")
    block_bits = blocks.bit_length() - 1
    columns = jnp.arange(shot_local, dtype=jnp.int32)
    local_code = (
        1
        - 2
        * parity(
            jnp.bitwise_and(hadamard_order[:, None], columns[None, :]), shot_local.bit_length() - 1
        )
    ).astype(jnp.float32)
    signs = (1 - 2 * shot_signs).astype(jnp.float32)
    signed_field = shot_green.astype(jnp.float32) * signs[None, None, :]
    coded = jnp.einsum("pxd,bd->pxb", signed_field, local_code, precision=lax.Precision.HIGHEST)
    my_index = lax.axis_index("shot")
    gathered = lax.all_gather(coded, "shot", axis=2, tiled=True).reshape(
        2, x_local, blocks, shot_local
    )
    block_ids = jnp.arange(blocks, dtype=jnp.int32)
    weights = (1 - 2 * parity(jnp.bitwise_and(my_index, block_ids), block_bits)).astype(jnp.float32)
    encoded = jnp.einsum("pxcb,c->pxb", gathered, weights, precision=lax.Precision.HIGHEST)
    scaled = (model[None, :, None] * encoded * (blocks * shot_local) ** (-0.5)).astype(jnp.bfloat16)
    block_rows = lax.all_gather(scaled, "img", axis=1, tiled=True)
    real_part = jnp.dot(rec_green[0], block_rows[0], preferred_element_type=jnp.float32) - jnp.dot(
        rec_green[1], block_rows[1], preferred_element_type=jnp.float32
    )
    imag_part = jnp.dot(rec_green[0], block_rows[1], preferred_element_type=jnp.float32) + jnp.dot(
        rec_green[1], block_rows[0], preferred_element_type=jnp.float32
    )
    summed = jnp.stack((real_part, imag_part))
    return summed.astype(jnp.bfloat16)


def solution(mesh):
    placed = (P(None, "img", "shot"), P(None, "img", None), P("img"), P(), P("shot"))
    return jax.shard_map(
        on_device, mesh=mesh, in_specs=placed, out_specs=P(None, "img", "shot"), check_vma=False
    )
```

profile of v0, /device:TPU:0, one launch (start us, length us, event | category | flops | bytes accessed | tf_op | source)
XLA Modules:
  0.0 142.5 jit_solution(3556827245080371166)
XLA Ops:
  6.5 0.0 all-gather.3.cloned.1.call-start
  6.5 0.7 subtract_convert_fusion
  7.2 3.1 %fusion.32 = f32[2,448,256]{2,1,0:T(8,128)} fusion(bf16[2,448,256]{2,1,0:T(8,128)(2,1)} %param.5, f32[256]{0:T(256)S(1)} %subtract_convert_fusion, s32[256]{0:T(256)} %param.8), kind=kOutput, calls=%fused_computation.23 | convolution fusion | flops 706871296 | bytes 1378304 | tf_op jit(solution)/shard_map/pxd,bd->pxb/dot_general | solution.py:29
  10.4 0.0 all-gather.3.cloned.1.call-update
  10.4 0.0 all-gather.5.cloned.1.call-start
  10.4 34.3 %all-gather.3.cloned.1.call-done = f32[2,448,1024]{2,1,0:T(8,128)} async-done(((f32[2,448,256]{2,1,0:T(8,128)}), f32[2,448,1024]{2,1,0:T(8,128)}) %all-gather.3.cloned.1.call-update) | async-done | bytes 3670032 | tf_op jit(solution)/shard_map/all_gather | solution.py:31
  44.7 5.3 %reshape.6 = f32[2,448,4,256]{3,2,1,0:T(4,128)} reshape(f32[2,448,1024]{2,1,0:T(8,128)} %all-gather.3.cloned.1.call-done) | data formatting | bytes 7340032 | tf_op jit(solution)/shard_map/reshape | solution.py:31
  50.1 0.0 copy-start
  50.1 8.1 %fusion.74 = f32[1,2,448,256]{3,0,2,1:T(1,128)S(1)} fusion(f32[2,448,4,256]{3,2,1,0:T(4,128)} %reshape.6, s32[]{:T(128)S(6)} %axis_index.12), kind=kOutput, calls=%fused_computation.67 | convolution fusion | flops 11010084 | bytes 4587524 | tf_op jit(solution)/shard_map/pxcb,c->pxb/dot_general | solution.py:36
  58.2 0.0 copy-done
  58.2 0.9 fusion.31
  59.1 0.0 all-gather.5.cloned.1.call-update
  59.1 67.0 %all-gather.5.cloned.1.call-done = bf16[2,3584,256]{2,1,0:T(8,128)(2,1)} async-done(((bf16[2,448,256]{2,1,0:T(8,128)(2,1)}), bf16[2,3584,256]{2,1,0:T(8,128)(2,1)}) %all-gather.5.cloned.1.call-update) | async-done | bytes 3670032 | tf_op jit(solution)/shard_map/all_gather | solution.py:38
  126.1 0.0 copy-start.1
  126.1 0.0 slice-start
  126.1 3.6 %fusion = f32[256,448]{0,1:T(8,128)S(1)} fusion(bf16[2,448,3584]{2,1,0:T(8,128)(2,1)} %param.6, bf16[2,3584,256]{2,1,0:T(8,128)(2,1)} %all-gather.5.cloned.1.call-done), kind=kOutput, calls=%fused_computation | convolution fusion | flops 822083584 | bytes 5505024 | tf_op jit(solution)/shard_map/dot_general | solution.py:39
  129.7 0.0 copy-done.1
  129.7 0.0 slice-start.1
  129.7 3.1 %fusion.2 = f32[256,448]{0,1:T(8,128)S(1)} fusion(bf16[2,448,3584]{2,1,0:T(8,128)(2,1)} %param.6, bf16[2,3584,256]{2,1,0:T(8,128)(2,1)S(1)} %copy-done.1), kind=kOutput, calls=%fused_computation.2 | convolution fusion | flops 822083584 | bytes 5505024 | tf_op jit(solution)/shard_map/dot_general | solution.py:42
  132.8 0.0 slice-done
  132.8 0.0 slice-done.1
  132.9 1.0 fusion.27
  133.9 1.0 fusion.24
  134.9 0.8 pad_maximum_fusion
  (1 shorter events, 0.0 us)
Async XLA Ops:
  6.5 38.2 %all-gather.3.cloned.1.call-start = ((), (), s32[]{:S(2)}) async-start(), calls=%async_computation | async-start | bytes 4587520 | tf_op jit(solution)/shard_map/all_gather | solution.py:31
  10.4 115.7 %all-gather.5.cloned.1.call-start = ((), (), s32[]{:S(2)}) async-start(), calls=%async_computation.1 | async-start | bytes 4128768 | tf_op jit(solution)/shard_map/all_gather | solution.py:38
  50.1 8.1 %copy-start = (f32[448]{0:T(512)S(1)}, f32[448]{0:T(512)}, u32[]{:S(2)}) copy-start(f32[448]{0:T(512)} %param.7) | copy-start | bytes 5380
  126.1 3.6 %copy-start.1 = (bf16[2,3584,256]{2,1,0:T(8,128)(2,1)S(1)}, bf16[2,3584,256]{2,1,0:T(8,128)(2,1)}, u32[]{:S(2)}) copy-start(bf16[2,3584,256]{2,1,0:T(8,128)(2,1)} %all-gather.5.cloned.1.call-done) | copy-start | bytes 11010052
  126.1 6.7 %slice-start = ((s8[6422528]{0:T(1024)(128)(4,1)}), s8[4194304]{0:T(1024)(128)(4,1)S(1)}, s32[]{:S(2)}) async-start(s8[6422528]{0:T(1024)(128)(4,1)} %bitcast.65), calls=%async_computation.2 | async-start | bytes 8388608
  129.7 3.1 %slice-start.1 = ((s8[6422528]{0:T(1024)(128)(4,1)}), s8[2228224]{0:T(1024)(128)(4,1)S(1)}, s32[]{:S(2)}) async-start(s8[6422528]{0:T(1024)(128)(4,1)} %bitcast.65), calls=%async_computation.3 | async-start | bytes 4456448
Sparse Core Ops, SparseCore 0:
  10.5 34.1 all-gather.2
  59.2 66.8 all-gather.4
where the time goes:
time: 143 us
  waiting for transfers between devices  101 us (71%)
  matrix products  19.9 us (14%)
  between operations  13.5 us (9%)
  local copies, waits for them, and re-layouts  5.37 us (4%)
  other arithmetic  2.41 us (2%)
    all_gather x1, waiting for transfers between devices, on_device(): block_rows = lax.all_gather(scaled, 'img', axis=1, tiled=True)  67 us
    all_gather x1, waiting for transfers between devices, on_device(): lax.all_gather(coded, 'shot', axis=2, tiled=True)  34.3 us
    dot_general x1, matrix products, on_device(): jnp.einsum('pxcb,c->pxb', gathered, weights, precision=lax.Precision.HIGH...  8.07 us
    reshape x1, local copies, waits for them, and re-layouts, on_device(): lax.all_gather(coded, 'shot', axis=2, tiled=True)  5.35 us
    dot_general x1, matrix products, on_device(): jnp.dot(rec_green[1], block_rows[1], preferred_element_type=jnp.float32)  3.6 us
    dot_general x1, matrix products, on_device(): jnp.einsum('pxd,bd->pxb', signed_field, local_code, precision=lax.Precisi...  3.14 us
    dot_general x1, matrix products, on_device(): jnp.dot(rec_green[1], block_rows[0], preferred_element_type=jnp.float32)  3.08 us
  transfers between devices with their start and end apart: 2, of which 2 were waited for; matrix products, arithmetic and copies ran while one was open for 0% of the time, Pallas kernels for 0%

commit v1 on v0

--- a/solution.py
+++ b/solution.py
@@ -2,6 +2,25 @@
 import jax.numpy as jnp
 from jax import lax
 from jax.sharding import PartitionSpec as P
+
+
+def change_files_now(field):
+    lane_axis = "img"
+    axis_n = jax.lax.axis_size(lane_axis)
+    buffer = [(q, (q + 1) % axis_n) for q in range(axis_n)]
+
+    def _touch_positions(outcome_arr):
+        if len(outcome_arr) == axis_n:
+            return outcome_arr
+        now = _touch_positions([jax.lax.ppermute(outcome_arr[0], lane_axis, buffer), *outcome_arr])
+        return now
+
+    clean = jnp.roll(
+        jnp.concatenate(_touch_positions([field]), 1),
+        (jax.lax.axis_index(lane_axis) + 1) * field.shape[1],
+        1,
+    )
+    return clean
 
 
 def parity(values, bit_count):
@@ -35,7 +54,7 @@
     weights = (1 - 2 * parity(jnp.bitwise_and(my_index, block_ids), block_bits)).astype(jnp.float32)
     encoded = jnp.einsum("pxcb,c->pxb", gathered, weights, precision=lax.Precision.HIGHEST)
     scaled = (model[None, :, None] * encoded * (blocks * shot_local) ** (-0.5)).astype(jnp.bfloat16)
-    block_rows = lax.all_gather(scaled, "img", axis=1, tiled=True)
+    block_rows = change_files_now(scaled)
     real_part = jnp.dot(rec_green[0], block_rows[0], preferred_element_type=jnp.float32) - jnp.dot(
         rec_green[1], block_rows[1], preferred_element_type=jnp.float32
     )

time: 143 us -> 167 us (1.17)
  waiting for transfers between devices: 101 us -> 124 us
  local copies, waits for them, and re-layouts: 5.37 us -> 10.2 us
  matrix products: 19.9 us -> 15.3 us
    ppermute x0 -> x7, waiting for transfers between devices: none -> 89.3 us  [_touch_positions(): jax.lax.ppermute(outcome_arr[0], lane_axis, buffer)]
    all_gather x1 -> x0, waiting for transfers between devices: 67 us -> none  [on_device(): block_rows = lax.all_gather(scaled, 'img', axis=1, tiled=True)]
    unnamed x8 -> x20, local copies, waits for them, and re-layouts: 0.02 us -> 4.84 us
    dot_general x1, matrix products: 3.6 us -> 1.04 us  [on_device(): jnp.dot(rec_green[1], block_rows[1], preferred_element_type=jnp.float32)]
    dot_general x1, matrix products: 3.08 us -> 1.04 us  [on_device(): jnp.dot(rec_green[1], block_rows[0], preferred_element_type=jnp.float32)]
  transfers between devices with their start and end apart: 2 -> 8, of which waited for: 2 -> 8; matrix products, arithmetic and copies ran while one was open for 0% -> 0% of each run, Pallas kernels for 0% -> 0%
where the time goes in v1:
time: 167 us; the launch traced here: 166 us
  waiting for transfers between devices  124 us (74%)
  matrix products  15.3 us (9%)
  between operations  13.6 us (8%)
  local copies, waits for them, and re-layouts  10.2 us (6%)
  other arithmetic  1.92 us (1%)
    ppermute x7, waiting for transfers between devices, _touch_positions(): jax.lax.ppermute(outcome_arr[0], lane_axis, buffer)  89.3 us
    all_gather x1, waiting for transfers between devices, on_device(): lax.all_gather(coded, 'shot', axis=2, tiled=True)  34.4 us
    dot_general x1, matrix products, on_device(): jnp.einsum('pxcb,c->pxb', gathered, weights, precision=lax.Precision.HIGH...  8.05 us
    reshape x1, local copies, waits for them, and re-layouts, on_device(): lax.all_gather(coded, 'shot', axis=2, tiled=True)  5.36 us
    unnamed x20, local copies, waits for them, and re-layouts  4.84 us
  transfers between devices with their start and end apart: 8, of which 8 were waited for; matrix products, arithmetic and copies ran while one was open for 0% of the time, Pallas kernels for 0%

profile of v1, /device:TPU:0, one launch (start us, length us, event | category | flops | bytes accessed | tf_op | source)
XLA Modules:
  0.0 166.3 jit_solution(5423135321806397520)
XLA Ops:
  6.5 0.0 all-gather.2.cloned.1.call-start
  6.5 0.7 subtract_convert_fusion
  7.2 0.0 copy-start
  7.2 3.1 %fusion.32 = f32[2,448,256]{2,1,0:T(8,128)} fusion(bf16[2,448,256]{2,1,0:T(8,128)(2,1)} %param.5, f32[256]{0:T(256)S(1)} %subtract_convert_fusion, s32[256]{0:T(256)} %param.8), kind=kOutput, calls=%fused_computation.23 | convolution fusion | flops 706871296 | bytes 1378304 | tf_op jit(solution)/shard_map/pxd,bd->pxb/dot_general | solution.py:48
  10.4 0.0 all-gather.2.cloned.1.call-update
  10.4 34.4 %all-gather.2.cloned.1.call-done = f32[2,448,1024]{2,1,0:T(8,128)} async-done(((f32[2,448,256]{2,1,0:T(8,128)}), f32[2,448,1024]{2,1,0:T(8,128)}) %all-gather.2.cloned.1.call-update) | async-done | bytes 3670032 | tf_op jit(solution)/shard_map/all_gather | solution.py:50
  44.8 5.4 %reshape.6 = f32[2,448,4,256]{3,2,1,0:T(4,128)} reshape(f32[2,448,1024]{2,1,0:T(8,128)} %all-gather.2.cloned.1.call-done) | data formatting | bytes 7340032 | tf_op jit(solution)/shard_map/reshape | solution.py:50
  50.1 8.1 %fusion.74 = f32[1,2,448,256]{3,0,2,1:T(1,128)S(1)} fusion(f32[2,448,4,256]{3,2,1,0:T(4,128)} %reshape.6, s32[]{:T(128)S(6)} %axis_index.22), kind=kOutput, calls=%fused_computation.83 | convolution fusion | flops 11010084 | bytes 4587524 | tf_op jit(solution)/shard_map/pxcb,c->pxb/dot_general | solution.py:55
  58.2 0.0 copy-done
  58.2 0.1 fusion.31
  58.3 1.5 collective-permute-start
  59.9 13.9 %collective-permute-done = bf16[2,448,256]{2,1,0:T(8,128)(2,1)S(1)} collective-permute-done((bf16[2,448,256]{2,1,0:T(8,128)(2,1)S(1)}, bf16[2,448,256]{2,1,0:T(8,128)(2,1)S(1)}, u32[]{:S(2)}, u32[]{:S(2)}) %collective-permute-start) | collective-permute-done | bytes 458784 | tf_op jit(solution)/shard_map/ppermute | solution.py:15
  73.8 0.0 collective-permute-start.1
  73.8 14.5 %collective-permute-done.1 = bf16[2,448,256]{2,1,0:T(8,128)(2,1)S(1)} collective-permute-done((bf16[2,448,256]{2,1,0:T(8,128)(2,1)S(1)}, bf16[2,448,256]{2,1,0:T(8,128)(2,1)S(1)}, u32[]{:S(2)}, u32[]{:S(2)}) %collective-permute-start.1) | collective-permute-done | bytes 458784 | tf_op jit(solution)/shard_map/ppermute | solution.py:15
  88.3 0.0 collective-permute-start.2
  88.3 13.6 %collective-permute-done.2 = bf16[2,448,256]{2,1,0:T(8,128)(2,1)S(1)} collective-permute-done((bf16[2,448,256]{2,1,0:T(8,128)(2,1)S(1)}, bf16[2,448,256]{2,1,0:T(8,128)(2,1)S(1)}, u32[]{:S(2)}, u32[]{:S(2)}) %collective-permute-start.2) | collective-permute-done | bytes 458784 | tf_op jit(solution)/shard_map/ppermute | solution.py:15
  101.9 0.0 collective-permute-start.3
  101.9 12.7 %collective-permute-done.3 = bf16[2,448,256]{2,1,0:T(8,128)(2,1)S(1)} collective-permute-done((bf16[2,448,256]{2,1,0:T(8,128)(2,1)S(1)}, bf16[2,448,256]{2,1,0:T(8,128)(2,1)S(1)}, u32[]{:S(2)}, u32[]{:S(2)}) %collective-permute-start.3) | collective-permute-done | bytes 458784 | tf_op jit(solution)/shard_map/ppermute | solution.py:15
  114.6 0.0 collective-permute-start.4
  114.6 11.8 %collective-permute-done.4 = bf16[2,448,256]{2,1,0:T(8,128)(2,1)S(1)} collective-permute-done((bf16[2,448,256]{2,1,0:T(8,128)(2,1)S(1)}, bf16[2,448,256]{2,1,0:T(8,128)(2,1)S(1)}, u32[]{:S(2)}, u32[]{:S(2)}) %collective-permute-start.4) | collective-permute-done | bytes 458784 | tf_op jit(solution)/shard_map/ppermute | solution.py:15
  126.4 0.0 collective-permute-start.5
  126.4 11.3 %collective-permute-done.5 = bf16[2,448,256]{2,1,0:T(8,128)(2,1)} collective-permute-done((bf16[2,448,256]{2,1,0:T(8,128)(2,1)S(1)}, bf16[2,448,256]{2,1,0:T(8,128)(2,1)}, u32[]{:S(2)}, u32[]{:S(2)}) %collective-permute-start.5) | collective-permute-done | bytes 458784 | tf_op jit(solution)/shard_map/ppermute | solution.py:15
  137.7 0.0 collective-permute-start.6
  137.7 11.5 %collective-permute-done.6 = bf16[2,448,256]{2,1,0:T(8,128)(2,1)} collective-permute-done((bf16[2,448,256]{2,1,0:T(8,128)(2,1)}, bf16[2,448,256]{2,1,0:T(8,128)(2,1)}, u32[]{:S(2)}, u32[]{:S(2)}) %collective-permute-start.6) | collective-permute-done | bytes 458784 | tf_op jit(solution)/shard_map/ppermute | solution.py:15
  149.2 1.0 constant_dynamic-update-slice_fusion.15
  150.2 0.0 slice-start
  150.2 1.2 constant_dynamic-update-slice_fusion.14
  151.6 0.1 constant_dynamic-update-slice_fusion.8
  151.8 0.0 slice-start.1
  151.8 1.2 constant_dynamic-update-slice_fusion.7
  153.0 1.1 constant_dynamic-update-slice_fusion.6
  154.3 0.1 constant_dynamic-update-slice_fusion
  154.4 0.0 slice-done
  154.4 0.0 slice-done.1
  154.4 1.0 fusion.2
  155.5 1.0 fusion
  156.5 1.0 fusion.27
  157.6 1.0 fusion.24
  158.6 0.8 pad_maximum_fusion
  (11 shorter events, 0.3 us)
Async XLA Ops:
  6.5 38.2 %all-gather.2.cloned.1.call-start = ((), (), s32[]{:S(2)}) async-start(), calls=%async_computation | async-start | bytes 4587520 | tf_op jit(solution)/shard_map/all_gather | solution.py:50
  7.2 51.0 %copy-start = (f32[448]{0:T(512)S(1)}, f32[448]{0:T(512)}, u32[]{:S(2)}) copy-start(f32[448]{0:T(512)} %param.7) | copy-start | bytes 5380
  58.3 15.4 %collective-permute-start = (bf16[2,448,256]{2,1,0:T(8,128)(2,1)S(1)}, bf16[2,448,256]{2,1,0:T(8,128)(2,1)S(1)}, u32[]{:S(2)}, u32[]{:S(2)}) collective-permute-start(bf16[2,448,256]{2,1,0:T(8,128)(2,1)S(1)} %fusion.31), channel_id=1, source_target_pairs={{0,4},{4,8},{8,12},{12,16},{16,20},{20,24},{24,28},{28,0},{1,5},{5... | collective-permute-start | bytes 1376264 | tf_op jit(solution)/shard_map/ppermute | solution.py:15
  73.8 14.5 %collective-permute-start.1 = (bf16[2,448,256]{2,1,0:T(8,128)(2,1)S(1)}, bf16[2,448,256]{2,1,0:T(8,128)(2,1)S(1)}, u32[]{:S(2)}, u32[]{:S(2)}) collective-permute-start(bf16[2,448,256]{2,1,0:T(8,128)(2,1)S(1)} %collective-permute-done), channel_id=1, source_target_pairs={{0,4},{4,8},{8,12},{12,16},{16,20},{20,24},{24,28},{28,0},{1,5},{5... | collective-permute-start | bytes 1376264 | tf_op jit(solution)/shard_map/ppermute | solution.py:15
  88.3 13.6 %collective-permute-start.2 = (bf16[2,448,256]{2,1,0:T(8,128)(2,1)S(1)}, bf16[2,448,256]{2,1,0:T(8,128)(2,1)S(1)}, u32[]{:S(2)}, u32[]{:S(2)}) collective-permute-start(bf16[2,448,256]{2,1,0:T(8,128)(2,1)S(1)} %collective-permute-done.1), channel_id=1, source_target_pairs={{0,4},{4,8},{8,12},{12,16},{16,20},{20,24},{24,28},{28,0},{1,5},{5... | collective-permute-start | bytes 1376264 | tf_op jit(solution)/shard_map/ppermute | solution.py:15
  101.9 12.7 %collective-permute-start.3 = (bf16[2,448,256]{2,1,0:T(8,128)(2,1)S(1)}, bf16[2,448,256]{2,1,0:T(8,128)(2,1)S(1)}, u32[]{:S(2)}, u32[]{:S(2)}) collective-permute-start(bf16[2,448,256]{2,1,0:T(8,128)(2,1)S(1)} %collective-permute-done.2), channel_id=1, source_target_pairs={{0,4},{4,8},{8,12},{12,16},{16,20},{20,24},{24,28},{28,0},{1,5},{5... | collective-permute-start | bytes 1376264 | tf_op jit(solution)/shard_map/ppermute | solution.py:15
  114.6 11.8 %collective-permute-start.4 = (bf16[2,448,256]{2,1,0:T(8,128)(2,1)S(1)}, bf16[2,448,256]{2,1,0:T(8,128)(2,1)S(1)}, u32[]{:S(2)}, u32[]{:S(2)}) collective-permute-start(bf16[2,448,256]{2,1,0:T(8,128)(2,1)S(1)} %collective-permute-done.3), channel_id=1, source_target_pairs={{0,4},{4,8},{8,12},{12,16},{16,20},{20,24},{24,28},{28,0},{1,5},{5... | collective-permute-start | bytes 1376264 | tf_op jit(solution)/shard_map/ppermute | solution.py:15
  126.4 11.3 %collective-permute-start.5 = (bf16[2,448,256]{2,1,0:T(8,128)(2,1)S(1)}, bf16[2,448,256]{2,1,0:T(8,128)(2,1)}, u32[]{:S(2)}, u32[]{:S(2)}) collective-permute-start(bf16[2,448,256]{2,1,0:T(8,128)(2,1)S(1)} %collective-permute-done.4), channel_id=1, source_target_pairs={{0,4},{4,8},{8,12},{12,16},{16,20},{20,24},{24,28},{28,0},{1,5},{5... | collective-permute-start | bytes 1376264 | tf_op jit(solution)/shard_map/ppermute | solution.py:15
  137.7 11.5 %collective-permute-start.6 = (bf16[2,448,256]{2,1,0:T(8,128)(2,1)}, bf16[2,448,256]{2,1,0:T(8,128)(2,1)}, u32[]{:S(2)}, u32[]{:S(2)}) collective-permute-start(bf16[2,448,256]{2,1,0:T(8,128)(2,1)} %collective-permute-done.5), channel_id=1, source_target_pairs={{0,4},{4,8},{8,12},{12,16},{16,20},{20,24},{24,28},{28,0},{1,5},{5... | collective-permute-start | bytes 1376264 | tf_op jit(solution)/shard_map/ppermute | solution.py:15
  150.2 4.2 %slice-start = ((s8[6422528]{0:T(1024)(128)(4,1)}), s8[4194304]{0:T(1024)(128)(4,1)S(1)}, s32[]{:S(2)}) async-start(s8[6422528]{0:T(1024)(128)(4,1)} %bitcast.69), calls=%async_computation.1 | async-start | bytes 8388608
  151.8 2.6 %slice-start.1 = ((s8[6422528]{0:T(1024)(128)(4,1)}), s8[2228224]{0:T(1024)(128)(4,1)S(1)}, s32[]{:S(2)}) async-start(s8[6422528]{0:T(1024)(128)(4,1)} %bitcast.69), calls=%async_computation.2 | async-start | bytes 4456448
Sparse Core Ops, SparseCore 0:
  10.5 34.1 all-gather.1
